TPU v7x, 512 devices: a whole 4x8x8 slice. The times are simulated.
512 devices in a mesh: gx: 16 (over y, core), gy: 32 (over x, z).
Axes of the slice: x: 4, y: 8, z: 8, core: 2. Of those that a mesh axis runs over, the one named last changes fastest.
Arguments:
- columns: float32 [262144, 512], P(('gx', 'gy')), may hold values from -6 to 6
- col_basis: float32 [262144, 128], P(('gx', 'gy')), may hold values from -0.25 to 0.25
- row_basis: float32 [262144, 128], P(('gx', 'gy')), may hold values from -0.5 to 0.5
- order_perm: int32 [512, 512], P(('gx', 'gy')), may hold values from 0 to 511, each once within a row
- near_blocks: float32 [2048, 5, 128, 128], P(('gx', 'gy')), may hold values from -0.25 to 0.25
- band_offsets: int32 [2048, 5], P(('gx', 'gy')), may hold values from -4 to 4
- transfer: float32 [8, 2, 128, 128], replicated, may hold values from -0.375 to 0.375
- coupling: float32 [9, 128, 128], replicated, may hold values from -0.5 to 0.5
Outputs:
- product: float32 [262144, 512], P(('gx', 'gy'))
Inputs may be any that keep to these rules, and one draw needn't show every extreme that they name: `order_perm`: each row is a permutation of the 512 rows of its leaf.
All inputs are finite; a program needn't handle non-finite values.
Results may differ from a plain program's by a relative error of at most 0.0001.
Values sent between devices are 32-bit elements; how exact they have to be, the bound alone decides.
A program may use at most 64 MiB of HBM per device.

v0:
```python
import jax
import jax.numpy as jnp
from jax import lax
from jax.sharding import PartitionSpec as P

BLK = 128
REACH = 4


def from_partner(x, axis, bit):
    return lax.ppermute(x, axis, [(i, i ^ 1 << bit) for i in range(lax.axis_size(axis))])


def extended(x, sides, width):
    for axis, dim in sides:
        size, length = (lax.axis_size(axis), x.shape[dim])
        up = [(i, (i + 1) % size) for i in range(size - 1)]
        down = [(j, i) for i, j in up]
        last = lax.slice_in_dim(x, length - width, length, axis=dim)
        initial = lax.slice_in_dim(x, 0, width, axis=dim)
        before = lax.ppermute(last, axis, up)
        after = lax.ppermute(initial, axis, down)
        x = jnp.concatenate([before, x, after], axis=dim)
    return x


def near_field(padded_rows, blocks_here, offsets_here):
    rhs_cols = padded_rows.shape[1]
    column_blocks = padded_rows.reshape(-1, BLK, rhs_cols)
    block_index = jnp.arange(offsets_here.shape[0], dtype=jnp.int32)[:, None] + offsets_here + REACH
    taken = column_blocks[block_index]
    result = jnp.einsum("jbrc,jbcn->jrn", blocks_here, taken, precision=lax.Precision.HIGHEST)
    return result.reshape(-1, rhs_cols)


def sibling_step(own_node, sibling, which_side, transfer, coupling, level, levels):
    exact = lax.Precision.HIGHEST
    on_left = which_side == 0
    left_node = jnp.where(on_left, own_node, sibling)
    right_node = jnp.where(on_left, sibling, own_node)
    chosen = jnp.where(on_left, coupling[level], coupling[level].T)
    coupled = jnp.dot(chosen, sibling, precision=exact)
    if level < levels - 1:
        parent = jnp.dot(transfer[level, 0].T, left_node, precision=exact) + jnp.dot(
            transfer[level, 1].T, right_node, precision=exact
        )
    else:
        parent = own_node
    return (coupled, parent)


def per_device(
    columns, col_basis, row_basis, order_perm, near_blocks, band_offsets, transfer, coupling
):
    exact = lax.Precision.HIGHEST
    across = lax.axis_size("gx")
    along = lax.axis_size("gy")
    high_bits = across.bit_length() - 1
    low_bits = along.bit_length() - 1
    levels = high_bits + low_bits
    index_x = lax.axis_index("gx")
    index_y = lax.axis_index("gy")
    leaf_index = index_x * along + index_y
    tree_cols = columns[order_perm[0]]
    skeleton = lax.dot_general(col_basis, tree_cols, (((0,), (0,)), ((), ())), precision=exact)
    couples = []
    for level in range(low_bits):
        sibling = from_partner(skeleton, "gy", level)
        which_side = index_y >> level & 1
        coupled, skeleton = sibling_step(
            skeleton, sibling, which_side, transfer, coupling, level, levels
        )
        couples.append(coupled)
    for bit_number in range(high_bits):
        level = low_bits + bit_number
        sibling = from_partner(skeleton, "gx", bit_number)
        which_side = index_x >> bit_number & 1
        coupled, skeleton = sibling_step(
            skeleton, sibling, which_side, transfer, coupling, level, levels
        )
        couples.append(coupled)
    expand = couples[levels - 1]
    for level in range(levels - 2, -1, -1):
        which_side = leaf_index >> level & 1
        chosen = jnp.where(which_side == 0, transfer[level, 0], transfer[level, 1])
        expand = couples[level] + jnp.dot(chosen, expand, precision=exact)
    far = jnp.dot(row_basis, expand, precision=exact)
    padded = extended(tree_cols, ((("gx", "gy"), 0),), REACH * BLK)
    near = near_field(padded, near_blocks, band_offsets)
    tree_out = near + far
    return jnp.zeros_like(tree_out).at[order_perm[0]].set(tree_out)


def solution(mesh):
    placed = (
        P(("gx", "gy"), None),
        P(("gx", "gy"), None),
        P(("gx", "gy"), None),
        P(("gx", "gy"), None),
        P(("gx", "gy"), None, None, None),
        P(("gx", "gy"), None),
        P(),
        P(),
    )
    return jax.shard_map(
        per_device, mesh=mesh, in_specs=placed, out_specs=P(("gx", "gy"), None), check_vma=False
    )
```

profile of v0, /device:TPU:57, one launch (start us, length us, event | category | flops | bytes accessed | tf_op | source)
XLA Modules:
  0.0 183.2 jit_solution(8334016896794118344)
XLA Ops:
  0.8 3.3 %gather_fusion = f32[512,512]{1,0:T(8,128)S(1)} fusion(f32[512,512]{1,0:T(8,128)} %param.8, s32[1024]{0:T(1024)S(1)} %pad_clamp_fusion.1), kind=kCustom, calls=%fused_computation | custom fusion | bytes 2099200 | tf_op jit(solution)/shard_map/gather | solution.py:64
  4.1 1.8 convolution_bitcast_fusion.1
  5.9 4.0 %collective-permute-start.2 = (f32[128,512]{0,1:T(8,128)S(1)}, f32[128,512]{0,1:T(8,128)S(1)}, u32[]{:S(2)}, u32[]{:S(2)}) collective-permute-start(f32[128,512]{0,1:T(8,128)S(1)} %convolution_bitcast_fusion.1), channel_id=1, source_target_pairs={{0,1},{1,0},{2,3},{3,2},{4,5},{5,4},{6,7},{7,6},{8,9},{9,8},{10,11... | collective-permute-start | bytes 786440 | tf_op jit(solution)/shard_map/ppermute | solution.py:11
  10.0 6.0 %collective-permute-done.2 = f32[128,512]{0,1:T(8,128)S(1)} collective-permute-done((f32[128,512]{0,1:T(8,128)S(1)}, f32[128,512]{0,1:T(8,128)S(1)}, u32[]{:S(2)}, u32[]{:S(2)}) %collective-permute-start.2) | collective-permute-done | bytes 262176 | tf_op jit(solution)/shard_map/ppermute | solution.py:11
  18.4 5.8 %collective-permute-start.3 = (f32[128,512]{0,1:T(8,128)S(1)}, f32[128,512]{0,1:T(8,128)S(1)}, u32[]{:S(2)}, u32[]{:S(2)}) collective-permute-start(f32[128,512]{0,1:T(8,128)S(1)} %fusion.8), channel_id=1, source_target_pairs={{0,2},{1,3},{2,0},{3,1},{4,6},{5,7},{6,4},{7,5},{8,10},{9,11},{10,... | collective-permute-start | bytes 786440 | tf_op jit(solution)/shard_map/ppermute | solution.py:11
  24.3 11.5 %collective-permute-done.3 = f32[128,512]{0,1:T(8,128)S(1)} collective-permute-done((f32[128,512]{0,1:T(8,128)S(1)}, f32[128,512]{0,1:T(8,128)S(1)}, u32[]{:S(2)}, u32[]{:S(2)}) %collective-permute-start.3) | collective-permute-done | bytes 262176 | tf_op jit(solution)/shard_map/ppermute | solution.py:11
  38.2 8.1 %collective-permute-start.4 = (f32[128,512]{0,1:T(8,128)S(1)}, f32[128,512]{0,1:T(8,128)S(1)}, u32[]{:S(2)}, u32[]{:S(2)}) collective-permute-start(f32[128,512]{0,1:T(8,128)S(1)} %fusion.7), channel_id=1, source_target_pairs={{0,4},{1,5},{2,6},{3,7},{4,0},{5,1},{6,2},{7,3},{8,12},{9,13},{10,... | collective-permute-start | bytes 786440 | tf_op jit(solution)/shard_map/ppermute | solution.py:11
  46.3 8.0 %collective-permute-done.4 = f32[128,512]{0,1:T(8,128)S(1)} collective-permute-done((f32[128,512]{0,1:T(8,128)S(1)}, f32[128,512]{0,1:T(8,128)S(1)}, u32[]{:S(2)}, u32[]{:S(2)}) %collective-permute-start.4) | collective-permute-done | bytes 262176 | tf_op jit(solution)/shard_map/ppermute | solution.py:11
  55.6 1.9 %fusion.6 = f32[128,512]{0,1:T(8,128)} fusion(f32[512,128]{1,0:T(8,128)S(1)} %fusion.26, f32[128,512]{0,1:T(8,128)S(1)} %fusion.7, f32[128,512]{0,1:T(8,128)S(1)} %collective-permute-done.4, pred[]{:T(512)S(6)} %eq.55, f32[8,2,128,128]{3,2,1,0:T(8,128)} %param.14), kind=kOutput, calls=%fused_computation.22 | convolution fusion | flops 100794368 | bytes 1114113 | tf_op jit(solution)/shard_map/dot_general | solution.py:44
  57.5 3.2 %collective-permute-start.5 = (f32[128,512]{0,1:T(8,128)}, f32[128,512]{0,1:T(8,128)S(1)}, u32[]{:S(2)}, u32[]{:S(2)}) collective-permute-start(f32[128,512]{0,1:T(8,128)} %fusion.6), channel_id=1, source_target_pairs={{0,8},{1,9},{2,10},{3,11},{4,12},{5,13},{6,14},{7,15},{8,0},{9,1},... | collective-permute-start | bytes 786440 | tf_op jit(solution)/shard_map/ppermute | solution.py:11
  60.7 4.2 %collective-permute-done.5 = f32[128,512]{0,1:T(8,128)S(1)} collective-permute-done((f32[128,512]{0,1:T(8,128)}, f32[128,512]{0,1:T(8,128)S(1)}, u32[]{:S(2)}, u32[]{:S(2)}) %collective-permute-start.5) | collective-permute-done | bytes 262176 | tf_op jit(solution)/shard_map/ppermute | solution.py:11
  66.2 2.0 %fusion.5 = f32[128,512]{0,1:T(8,128)} fusion(f32[512,128]{1,0:T(8,128)S(1)} %fusion.23, f32[128,512]{0,1:T(8,128)} %fusion.6, f32[128,512]{0,1:T(8,128)S(1)} %collective-permute-done.5, pred[]{:T(512)S(6)} %eq.57, f32[8,2,128,128]{3,2,1,0:T(8,128)} %param.14), kind=kOutput, calls=%fused_computation.19 | convolution fusion | flops 100794368 | bytes 1114113 | tf_op jit(solution)/shard_map/dot_general | solution.py:44
  68.2 4.6 %collective-permute-start.6 = (f32[128,512]{0,1:T(8,128)}, f32[128,512]{0,1:T(8,128)S(1)}, u32[]{:S(2)}, u32[]{:S(2)}) collective-permute-start(f32[128,512]{0,1:T(8,128)} %fusion.5), channel_id=1, source_target_pairs={{0,16},{1,17},{2,18},{3,19},{4,20},{5,21},{6,22},{7,23},{8,24},{9,... | collective-permute-start | bytes 786440 | tf_op jit(solution)/shard_map/ppermute | solution.py:11
  72.9 4.2 %collective-permute-done.6 = f32[128,512]{0,1:T(8,128)S(1)} collective-permute-done((f32[128,512]{0,1:T(8,128)}, f32[128,512]{0,1:T(8,128)S(1)}, u32[]{:S(2)}, u32[]{:S(2)}) %collective-permute-start.6) | collective-permute-done | bytes 262176 | tf_op jit(solution)/shard_map/ppermute | solution.py:11
  78.3 2.0 %fusion.4 = f32[128,512]{0,1:T(8,128)} fusion(f32[512,128]{1,0:T(8,128)S(1)} %fusion.20, f32[128,512]{0,1:T(8,128)} %fusion.5, f32[128,512]{0,1:T(8,128)S(1)} %collective-permute-done.6, pred[]{:T(512)S(6)} %eq.59, f32[8,2,128,128]{3,2,1,0:T(8,128)} %param.14), kind=kOutput, calls=%fused_computation.16 | convolution fusion | flops 100794368 | bytes 1114113 | tf_op jit(solution)/shard_map/dot_general | solution.py:44
  80.3 9.1 %collective-permute-start.7 = (f32[128,512]{0,1:T(8,128)}, f32[128,512]{0,1:T(8,128)}, u32[]{:S(2)}, u32[]{:S(2)}) collective-permute-start(f32[128,512]{0,1:T(8,128)} %fusion.4), channel_id=1, source_target_pairs={{0,32},{32,0},{64,96},{96,64},{128,160},{160,128},{192,224},{224,1... | collective-permute-start | bytes 786440 | tf_op jit(solution)/shard_map/ppermute | solution.py:11
  89.4 8.5 %collective-permute-start.1 = (f32[512,512]{1,0:T(8,128)S(1)}, f32[512,512]{1,0:T(8,128)}, u32[]{:S(2)}, u32[]{:S(2)}) collective-permute-start(f32[512,512]{1,0:T(8,128)S(1)} %gather_fusion), channel_id=1, source_target_pairs={{1,0},{2,1},{3,2},{4,3},{5,4},{6,5},{7,6},{8,7},{9,8},{10,9},{11,1... | collective-permute-start | bytes 3145736 | tf_op jit(solution)/shard_map/ppermute | solution.py:22
  98.0 1.9 %collective-permute-start = (f32[512,512]{1,0:T(8,128)S(1)}, f32[512,512]{1,0:T(8,128)}, u32[]{:S(2)}, u32[]{:S(2)}) collective-permute-start(f32[512,512]{1,0:T(8,128)S(1)} %gather_fusion), channel_id=1, source_target_pairs={{0,1},{1,2},{2,3},{3,4},{4,5},{5,6},{6,7},{7,8},{8,9},{9,10},{10,1... | collective-permute-start | bytes 3145736 | tf_op jit(solution)/shard_map/ppermute | solution.py:21
  101.4 2.0 %fusion.3 = f32[128,512]{0,1:T(8,128)} fusion(f32[512,128]{1,0:T(8,128)S(1)} %fusion.17, f32[128,512]{0,1:T(8,128)} %fusion.4, f32[128,512]{0,1:T(8,128)} %collective-permute-done.7, pred[]{:T(512)S(6)} %eq.61, f32[8,2,128,128]{3,2,1,0:T(8,128)} %param.14), kind=kOutput, calls=%fused_computation.13 | convolution fusion | flops 100794368 | bytes 1114113 | tf_op jit(solution)/shard_map/dot_general | solution.py:44
  103.4 3.0 %collective-permute-start.8 = (f32[128,512]{0,1:T(8,128)}, f32[128,512]{0,1:T(8,128)}, u32[]{:S(2)}, u32[]{:S(2)}) collective-permute-start(f32[128,512]{0,1:T(8,128)} %fusion.3), channel_id=1, source_target_pairs={{0,64},{32,96},{64,0},{96,32},{128,192},{160,224},{192,128},{224,1... | collective-permute-start | bytes 786440 | tf_op jit(solution)/shard_map/ppermute | solution.py:11
  108.1 1.6 copy.25
  112.8 1.6 copy.22
  116.0 1.6 copy.27
  121.8 3.7 %collective-permute-start.9 = (f32[128,512]{0,1:T(8,128)S(1)}, f32[128,512]{0,1:T(8,128)S(1)}, u32[]{:S(2)}, u32[]{:S(2)}) collective-permute-start(f32[128,512]{0,1:T(8,128)S(1)} %fusion.2), channel_id=1, source_target_pairs={{0,128},{32,160},{64,192},{96,224},{128,0},{160,32},{192,64},{224,... | collective-permute-start | bytes 786440 | tf_op jit(solution)/shard_map/ppermute | solution.py:11
  125.6 3.2 %collective-permute-done = f32[512,512]{1,0:T(8,128)} collective-permute-done((f32[512,512]{1,0:T(8,128)S(1)}, f32[512,512]{1,0:T(8,128)}, u32[]{:S(2)}, u32[]{:S(2)}) %collective-permute-start) | collective-permute-done | bytes 1048608 | tf_op jit(solution)/shard_map/ppermute | solution.py:21
  128.7 3.5 %pad_maximum_fusion = f32[1536,512]{1,0:T(8,128)} fusion(f32[512,512]{1,0:T(8,128)} %collective-permute-done.1, f32[512,512]{1,0:T(8,128)S(1)} %gather_fusion, f32[512,512]{1,0:T(8,128)} %collective-permute-done), kind=kLoop, calls=%fused_computation.3 | loop fusion | flops 1572864 | bytes 6291456 | tf_op jit(solution)/shard_map/concatenate | solution.py:23
  132.3 5.1 %gather_fusion.1 = f32[20,128,512]{2,1,0:T(8,128)} fusion(f32[12,128,512]{2,1,0:T(8,128)} %bitcast.225, s32[1024]{0:T(1024)S(1)} %pad_clamp_fusion), kind=kCustom, calls=%fused_computation.1 | custom fusion | bytes 10485840 | tf_op jit(solution)/shard_map/gather | solution.py:31
  139.6 1.9 %fusion.1 = f32[128,512]{0,1:T(8,128)} fusion(f32[512,128]{1,0:T(8,128)S(1)} %fusion.11, f32[128,512]{0,1:T(8,128)S(1)} %fusion.2, f32[128,512]{0,1:T(8,128)S(1)} %collective-permute-done.9, pred[]{:T(512)S(6)} %eq.65, f32[8,2,128,128]{3,2,1,0:T(8,128)} %param.14), kind=kOutput, calls=%fused_computation.7 | convolution fusion | flops 100794368 | bytes 1114113 | tf_op jit(solution)/shard_map/dot_general | solution.py:44
  141.5 3.7 %collective-permute-start.10 = (f32[128,512]{0,1:T(8,128)}, f32[128,512]{0,1:T(8,128)}, u32[]{:S(2)}, u32[]{:S(2)}) collective-permute-start(f32[128,512]{0,1:T(8,128)} %fusion.1), channel_id=1, source_target_pairs={{0,256},{32,288},{64,320},{96,352},{128,384},{160,416},{192,448},{... | collective-permute-start | bytes 786440 | tf_op jit(solution)/shard_map/ppermute | solution.py:11
  145.2 5.2 %fusion.133 = f32[4,512,128,1]{1,2,3,0:T(8,128)S(1)} fusion(f32[4,5,128,512]{3,2,1,0:T(8,128)} %bitcast.226, f32[4,5,128,128]{3,2,1,0:T(8,128)S(1)} %copy-done), kind=kOutput, calls=%fused_computation.185 | convolution fusion | flops 2013265920 | bytes 7602176 | tf_op jit(solution)/shard_map/jbrc,jbcn->jrn/dot_general | solution.py:32
  150.8 9.9 %collective-permute-done.10 = f32[128,512]{0,1:T(8,128)} collective-permute-done((f32[128,512]{0,1:T(8,128)}, f32[128,512]{0,1:T(8,128)}, u32[]{:S(2)}, u32[]{:S(2)}) %collective-permute-start.10) | collective-permute-done | bytes 262176 | tf_op jit(solution)/shard_map/ppermute | solution.py:11
  179.9 3.2 %scatter_custom_fusion = f32[512,512]{1,0:T(8,128)} fusion(s32[512]{0:T(512)S(1)} %bitcast.229, f32[512,512]{1,0:T(8,128)S(1)} %copy.29, f32[]{:T(128)} %constant.15.clone.1), kind=kCustom, calls=%fused_computation.31 | custom fusion | bytes 1048580 | tf_op jit(solution)/shard_map/scatter | solution.py:91
  (89 shorter events, 43.0 us)
Async XLA Ops:
  0.0 145.2 %copy-start = (f32[4,5,128,128]{3,2,1,0:T(8,128)S(1)}, f32[4,5,128,128]{3,2,1,0:T(8,128)}, u32[]{:S(2)}) copy-start(f32[4,5,128,128]{3,2,1,0:T(8,128)} %param.12) | copy-start | bytes 3932164
  0.8 3.3 %copy-start.19 = (f32[512,128]{1,0:T(8,128)S(1)}, f32[512,128]{1,0:T(8,128)}, u32[]{:S(2)}) copy-start(f32[512,128]{1,0:T(8,128)} %param.9) | copy-start | bytes 786436
  5.9 10.0 %collective-permute-start.2 = (f32[128,512]{0,1:T(8,128)S(1)}, f32[128,512]{0,1:T(8,128)S(1)}, u32[]{:S(2)}, u32[]{:S(2)}) collective-permute-start(f32[128,512]{0,1:T(8,128)S(1)} %convolution_bitcast_fusion.1), channel_id=1, source_target_pairs={{0,1},{1,0},{2,3},{3,2},{4,5},{5,4},{6,7},{7,6},{8,9},{9,8},{10,11... | collective-permute-start | bytes 786440 | tf_op jit(solution)/shard_map/ppermute | solution.py:11
  16.0 39.6 %copy-start.3 = (f32[128,512]{0,1:T(8,128)}, f32[128,512]{0,1:T(8,128)S(1)}, u32[]{:S(2)}) copy-start(f32[128,512]{0,1:T(8,128)S(1)} %collective-permute-done.2) | copy-start | bytes 786436
  18.4 17.3 %collective-permute-start.3 = (f32[128,512]{0,1:T(8,128)S(1)}, f32[128,512]{0,1:T(8,128)S(1)}, u32[]{:S(2)}, u32[]{:S(2)}) collective-permute-start(f32[128,512]{0,1:T(8,128)S(1)} %fusion.8), channel_id=1, source_target_pairs={{0,2},{1,3},{2,0},{3,1},{4,6},{5,7},{6,4},{7,5},{8,10},{9,11},{10,... | collective-permute-start | bytes 786440 | tf_op jit(solution)/shard_map/ppermute | solution.py:11
  35.7 19.9 %copy-start.5 = (f32[128,512]{0,1:T(8,128)}, f32[128,512]{0,1:T(8,128)S(1)}, u32[]{:S(2)}) copy-start(f32[128,512]{0,1:T(8,128)S(1)} %collective-permute-done.3) | copy-start | bytes 786436
  38.2 61.8 %copy-start.20 = (s32[4,5]{1,0:T(4,128)S(1)}, s32[4,5]{1,0:T(4,128)}, u32[]{:S(2)}) copy-start(s32[4,5]{1,0:T(4,128)} %param.13) | copy-start | bytes 244
  38.2 16.1 %collective-permute-start.4 = (f32[128,512]{0,1:T(8,128)S(1)}, f32[128,512]{0,1:T(8,128)S(1)}, u32[]{:S(2)}, u32[]{:S(2)}) collective-permute-start(f32[128,512]{0,1:T(8,128)S(1)} %fusion.7), channel_id=1, source_target_pairs={{0,4},{1,5},{2,6},{3,7},{4,0},{5,1},{6,2},{7,3},{8,12},{9,13},{10,... | collective-permute-start | bytes 786440 | tf_op jit(solution)/shard_map/ppermute | solution.py:11
  54.3 1.3 copy-start.7
  57.5 48.9 %copy-start.1 = (f32[9,128,128]{2,1,0:T(8,128)S(1)}, f32[9,128,128]{2,1,0:T(8,128)}, u32[]{:S(2)}) copy-start(f32[9,128,128]{2,1,0:T(8,128)} %param.15) | copy-start | bytes 1769476
  57.5 7.4 %collective-permute-start.5 = (f32[128,512]{0,1:T(8,128)}, f32[128,512]{0,1:T(8,128)S(1)}, u32[]{:S(2)}, u32[]{:S(2)}) collective-permute-start(f32[128,512]{0,1:T(8,128)} %fusion.6), channel_id=1, source_target_pairs={{0,8},{1,9},{2,10},{3,11},{4,12},{5,13},{6,14},{7,15},{8,0},{9,1},... | collective-permute-start | bytes 786440 | tf_op jit(solution)/shard_map/ppermute | solution.py:11
  65.0 42.2 %copy-start.9 = (f32[128,512]{0,1:T(8,128)}, f32[128,512]{0,1:T(8,128)S(1)}, u32[]{:S(2)}) copy-start(f32[128,512]{0,1:T(8,128)S(1)} %collective-permute-done.5) | copy-start | bytes 786436
  68.2 8.8 %collective-permute-start.6 = (f32[128,512]{0,1:T(8,128)}, f32[128,512]{0,1:T(8,128)S(1)}, u32[]{:S(2)}, u32[]{:S(2)}) collective-permute-start(f32[128,512]{0,1:T(8,128)} %fusion.5), channel_id=1, source_target_pairs={{0,16},{1,17},{2,18},{3,19},{4,20},{5,21},{6,22},{7,23},{8,24},{9,... | collective-permute-start | bytes 786440 | tf_op jit(solution)/shard_map/ppermute | solution.py:11
  77.1 42.0 %copy-start.11 = (f32[128,512]{0,1:T(8,128)}, f32[128,512]{0,1:T(8,128)S(1)}, u32[]{:S(2)}) copy-start(f32[128,512]{0,1:T(8,128)S(1)} %collective-permute-done.6) | copy-start | bytes 786436
  80.3 19.7 %collective-permute-start.7 = (f32[128,512]{0,1:T(8,128)}, f32[128,512]{0,1:T(8,128)}, u32[]{:S(2)}, u32[]{:S(2)}) collective-permute-start(f32[128,512]{0,1:T(8,128)} %fusion.4), channel_id=1, source_target_pairs={{0,32},{32,0},{64,96},{96,64},{128,160},{160,128},{192,224},{224,1... | collective-permute-start | bytes 786440 | tf_op jit(solution)/shard_map/ppermute | solution.py:11
  89.4 36.1 %collective-permute-start.1 = (f32[512,512]{1,0:T(8,128)S(1)}, f32[512,512]{1,0:T(8,128)}, u32[]{:S(2)}, u32[]{:S(2)}) collective-permute-start(f32[512,512]{1,0:T(8,128)S(1)} %gather_fusion), channel_id=1, source_target_pairs={{1,0},{2,1},{3,2},{4,3},{5,4},{6,5},{7,6},{8,7},{9,8},{10,9},{11,1... | collective-permute-start | bytes 3145736 | tf_op jit(solution)/shard_map/ppermute | solution.py:22
  98.0 30.8 %collective-permute-start = (f32[512,512]{1,0:T(8,128)S(1)}, f32[512,512]{1,0:T(8,128)}, u32[]{:S(2)}, u32[]{:S(2)}) collective-permute-start(f32[512,512]{1,0:T(8,128)S(1)} %gather_fusion), channel_id=1, source_target_pairs={{0,1},{1,2},{2,3},{3,4},{4,5},{5,6},{6,7},{7,8},{8,9},{9,10},{10,1... | collective-permute-start | bytes 3145736 | tf_op jit(solution)/shard_map/ppermute | solution.py:21
  103.4 15.7 %collective-permute-start.8 = (f32[128,512]{0,1:T(8,128)}, f32[128,512]{0,1:T(8,128)}, u32[]{:S(2)}, u32[]{:S(2)}) collective-permute-start(f32[128,512]{0,1:T(8,128)} %fusion.3), channel_id=1, source_target_pairs={{0,64},{32,96},{64,0},{96,32},{128,192},{160,224},{192,128},{224,1... | collective-permute-start | bytes 786440 | tf_op jit(solution)/shard_map/ppermute | solution.py:11
  121.8 16.5 %collective-permute-start.9 = (f32[128,512]{0,1:T(8,128)S(1)}, f32[128,512]{0,1:T(8,128)S(1)}, u32[]{:S(2)}, u32[]{:S(2)}) collective-permute-start(f32[128,512]{0,1:T(8,128)S(1)} %fusion.2), channel_id=1, source_target_pairs={{0,128},{32,160},{64,192},{96,224},{128,0},{160,32},{192,64},{224,... | collective-permute-start | bytes 786440 | tf_op jit(solution)/shard_map/ppermute | solution.py:11
  138.3 6.8 %copy-start.13 = (f32[128,512]{0,1:T(8,128)}, f32[128,512]{0,1:T(8,128)S(1)}, u32[]{:S(2)}) copy-start(f32[128,512]{0,1:T(8,128)S(1)} %collective-permute-done.9) | copy-start | bytes 786436
  141.5 19.2 %collective-permute-start.10 = (f32[128,512]{0,1:T(8,128)}, f32[128,512]{0,1:T(8,128)}, u32[]{:S(2)}, u32[]{:S(2)}) collective-permute-start(f32[128,512]{0,1:T(8,128)} %fusion.1), channel_id=1, source_target_pairs={{0,256},{32,288},{64,320},{96,352},{128,384},{160,416},{192,448},{... | collective-permute-start | bytes 786440 | tf_op jit(solution)/shard_map/ppermute | solution.py:11
  150.8 18.0 %copy-start.2 = (f32[9,128,128]{2,1,0:T(8,128)S(1)}, f32[9,128,128]{2,1,0:T(8,128)}, u32[]{:S(2)}) copy-start(f32[9,128,128]{2,1,0:T(8,128)} %param.15) | copy-start | bytes 1769476
  150.8 18.0 %copy-start.18 = (f32[128,128]{0,1:T(8,128)S(1)}, f32[128,128]{0,1:T(8,128)}, u32[]{:S(2)}) copy-start(f32[128,128]{0,1:T(8,128)} %copy.24) | copy-start | bytes 196612
  150.8 20.7 %copy-start.12 = (f32[128,512]{0,1:T(8,128)S(1)}, f32[128,512]{0,1:T(8,128)}, u32[]{:S(2)}) copy-start(f32[128,512]{0,1:T(8,128)} %copy-done.11) | copy-start | bytes 786436
  150.8 20.7 %copy-start.17 = (f32[128,128]{0,1:T(8,128)S(1)}, f32[128,128]{0,1:T(8,128)}, u32[]{:S(2)}) copy-start(f32[128,128]{0,1:T(8,128)} %copy.23) | copy-start | bytes 196612
  163.4 9.8 %copy-start.10 = (f32[128,512]{0,1:T(8,128)S(1)}, f32[128,512]{0,1:T(8,128)}, u32[]{:S(2)}) copy-start(f32[128,512]{0,1:T(8,128)} %copy-done.9) | copy-start | bytes 786436
  163.4 9.8 %copy-start.16 = (f32[128,128]{0,1:T(8,128)S(1)}, f32[128,128]{0,1:T(8,128)}, u32[]{:S(2)}) copy-start(f32[128,128]{0,1:T(8,128)} %copy.22) | copy-start | bytes 196612
  166.1 8.8 %copy-start.8 = (f32[128,512]{0,1:T(8,128)S(1)}, f32[128,512]{0,1:T(8,128)}, u32[]{:S(2)}) copy-start(f32[128,512]{0,1:T(8,128)} %copy-done.7) | copy-start | bytes 786436
  166.1 8.8 %copy-start.15 = (f32[128,128]{0,1:T(8,128)S(1)}, f32[128,128]{0,1:T(8,128)}, u32[]{:S(2)}) copy-start(f32[128,128]{0,1:T(8,128)} %copy.21) | copy-start | bytes 196612
  168.8 7.7 %copy-start.6 = (f32[128,512]{0,1:T(8,128)S(1)}, f32[128,512]{0,1:T(8,128)}, u32[]{:S(2)}) copy-start(f32[128,512]{0,1:T(8,128)} %copy-done.5) | copy-start | bytes 786436
  171.5 6.7 %copy-start.4 = (f32[128,512]{0,1:T(8,128)S(1)}, f32[128,512]{0,1:T(8,128)}, u32[]{:S(2)}) copy-start(f32[128,512]{0,1:T(8,128)} %copy-done.3) | copy-start | bytes 786436
  171.9 6.7 %copy-start.14 = (f32[512,128]{1,0:T(8,128)S(1)}, f32[512,128]{1,0:T(8,128)}, u32[]{:S(2)}) copy-start(f32[512,128]{1,0:T(8,128)} %param.10) | copy-start | bytes 786436
where the time goes:
time: 185 us; the launch traced here: 183 us
  starting transfers between devices  55.6 us (30%)
  matrix products  49.4 us (27%)
  waiting for transfers between devices  47.9 us (26%)
  local copies, waits for them, and re-layouts  25.2 us (14%)
  other arithmetic  4.36 us (2%)
    ppermute x9, starting transfers between devices, from_partner(): lax.ppermute(x, axis, [(i, i ^ 1 << bit) for i in range(lax.axis_size(axi...  45.2 us
    ppermute x9, waiting for transfers between devices, from_partner(): lax.ppermute(x, axis, [(i, i ^ 1 << bit) for i in range(lax.axis_size(axi...  44.7 us
    dot_general x8, matrix products, sibling_step(): jnp.dot(transfer[level, 0].T, left_node, precision=exact)  13.6 us
    squeeze x10, local copies, waits for them, and re-layouts, sibling_step(): chosen = jnp.where(on_left, coupling[level], coupling[level].T)  12.7 us
    dot_general x8, matrix products, sibling_step(): jnp.dot(transfer[level, 1].T, right_node, precision=exact)  10.1 us
    dot_general x8, matrix products, per_device(): expand = couples[level] + jnp.dot(chosen, expand, precision=exact)  9.95 us
    ppermute x1, starting transfers between devices, extended(): after = lax.ppermute(initial, axis, down)  8.52 us
    dot_general x9, matrix products, sibling_step(): coupled = jnp.dot(chosen, sibling, precision=exact)  7.6 us
  transfers between devices with their start and end apart: 11, of which 8 were waited for; matrix products, arithmetic and copies ran while one was open for 18% of the time, Pallas kernels for 0%

commit v1 on v0

v1 whole, which is shorter than its diff:
```python
import jax
import jax.numpy as jnp
from jax import lax
from jax.experimental import pallas as pl
from jax.experimental.pallas import tpu as pltpu
from jax.sharding import PartitionSpec as P

LEAF = 512
NRHS = 512
R = 128
BLK = 128
REACH = 4
NBAND = 5
NBLK = LEAF // BLK

NZ = 8
NX = 4
NC = 2
NY = 8

CW = 128
MESH = pl.DeviceIdType.MESH
F32 = jnp.float32
BF16 = jnp.bfloat16


def log2(n):
    return n.bit_length() - 1


def mm(a, b):
    return lax.dot_general(a, b, (((1,), (0,)), ((), ())), preferred_element_type=F32)


def split(x):
    high = x.astype(BF16)
    low = (x - high.astype(F32)).astype(BF16)
    return high, low


def lanes(parts):
    return jnp.concatenate(parts, axis=1)


def rows(parts):
    return jnp.concatenate(parts, axis=0)


def wide(x):
    return lanes(split(x))


def halves(x):
    half = x.shape[1] // 2
    return x[:, :half] + x[:, half:]


def kernel(
    x_hbm, v_hbm, u_hbm, perm_hbm, near_hbm, off_hbm, transfer_hbm, coupling_hbm, out_hbm,
    x_v, v_v, u_v, perm_v, near_v, off_s, transfer_v, coupling_v,
    up_w, down_w, coup_w, band, turned_band, near_w, far_w, turned, straight, total, out_v,
    skel, z_in, x_out, x_in, y_out, y_in, top, xr_out, xr_in, zr_out, zr_in,
    raw, perm_in,
    load_sem, store_sem,
    z_send, z_recv, x_send, x_recv, y_send, y_recv, xr_send, xr_recv, zr_send, zr_recv,
    halo_send, halo_recv, perm_send, perm_recv,
):
    nxc = NX * NC
    gx = lax.axis_index("gx")
    gy = lax.axis_index("gy")
    y, core = lax.div(gx, NC), lax.rem(gx, NC)
    xx, z = lax.div(gy, NZ), lax.rem(gy, NZ)
    along = NX * NZ
    leaves = along * NC * NY
    leaf = gx * along + gy
    xc = core * NX + xx
    levels = coupling_hbm.shape[0]
    chunks = NRHS // CW
    cz = NRHS // NZ
    cx = cz // nxc

    def z_dev(k):
        return (gx, xx * NZ + k)

    def x_dev(k):
        return (y * NC + lax.div(k, NX), lax.rem(k, NX) * NZ + z)

    def y_dev(k):
        return (k * NC + core, gy)

    def leaf_dev(k):
        return (lax.div(k, along), lax.rem(k, along))

    right = leaf_dev(lax.rem(leaf + 1, leaves))
    left = leaf_dev(lax.rem(leaf + leaves - 1, leaves))

    def remote(src, dst, send, recv, dev):
        return pltpu.make_async_remote_copy(
            src_ref=src, dst_ref=dst, send_sem=send, recv_sem=recv, device_id=dev, device_id_type=MESH
        )

    loads = [
        pltpu.make_async_copy(src, dst, load_sem.at[i])
        for i, (src, dst) in enumerate(
            (
                (perm_hbm, perm_v),
                (v_hbm, v_v),
                (x_hbm, x_v),
                (transfer_hbm, transfer_v),
                (coupling_hbm, coupling_v),
                (near_hbm, near_v),
                (u_hbm, u_v),
                (off_hbm, off_s),
            )
        )
    ]
    for load in loads:
        load.start()

    barrier = pltpu.get_barrier_semaphore()
    greeted = (
        [z_dev(lax.rem(z + k, NZ)) for k in range(1, NZ)]
        + [x_dev(lax.rem(xc + k, nxc)) for k in range(1, nxc)]
        + [y_dev(lax.rem(y + k, NY)) for k in range(1, NY)]
        + [left, right]
    )
    for dev in greeted:
        pl.semaphore_signal(barrier, inc=1, device_id=dev, device_id_type=MESH)
    pl.semaphore_wait(barrier, len(greeted))

    def halo(side, chunk):
        return remote(
            x_hbm.at[:, pl.ds(chunk * CW, CW)],
            raw.at[side, chunk],
            halo_send.at[side, chunk],
            halo_recv.at[side, chunk],
            (right, left)[side],
        )

    def halo_perm(side):
        return remote(
            perm_hbm, perm_in.at[side], perm_send.at[side], perm_recv.at[side], (right, left)[side]
        )

    for side in range(2):
        halo_perm(side).start()
        halo(side, 0).start()

    loads[0].wait()
    perm_row = perm_v[...]
    hit = lax.broadcasted_iota(jnp.int32, (LEAF, LEAF), 0) == perm_row
    turned[...] = jnp.where(hit, 1.0, 0.0).astype(BF16)
    loads[1].wait()
    basis = mm(turned[...], wide(v_v[...]))
    basis_t = basis.T.astype(BF16)
    loads[2].wait()
    for c in range(chunks):
        x_wide = wide(x_v[:, c * CW : (c + 1) * CW])
        s = mm(basis_t, x_wide)
        s = halves(s)
        s = s[:R] + s[R:]
        skel[c * CW : (c + 1) * CW, :] = s.T

    def z_copy(k):
        to = lax.rem(z + k, NZ)
        return remote(
            skel.at[pl.ds(to * cz, cz), :], z_in.at[z], z_send.at[k], z_recv.at[k], z_dev(to)
        )

    for k in range(1, NZ):
        z_copy(k).start()
    z_in[z] = skel[pl.ds(z * cz, cz), :]
    for chunk in range(1, chunks):
        for side in range(2):
            halo(side, chunk).start()

    loads[3].wait()
    loads[4].wait()

    def prepare(m, _):
        up_w[m] = wide(transfer_v[m])
        w = transfer_v[m]
        w = wide(lanes([w[:R].T, w[R:].T]))
        down_w[m] = rows([w, w])
        return 0

    lax.fori_loop(0, levels - 1, prepare, 0)

    def prepare_coupling(m, _):
        c = coupling_v[m]
        w = wide(c.T)
        coup_w[m, 0] = rows([w, w])
        w = wide(c)
        coup_w[m, 1] = rows([w, w])
        return 0

    lax.fori_loop(0, levels, prepare_coupling, 0)

    loads[5].wait()
    loads[7].wait()
    band[...] = jnp.zeros(band.shape, BF16)

    def fill_band(b, _):
        at_rows = pl.ds(pl.multiple_of(b * BLK, BLK), BLK)
        for offset in range(2 * REACH + 1):
            block = jnp.zeros((BLK, BLK), F32)
            for j in range(NBAND):
                here = jnp.where(off_s[b, j] == offset - REACH, 1.0, 0.0).astype(F32)
                block = block + near_v[b, j] * here
            at_lanes = pl.ds(pl.multiple_of((b + offset) * BLK, BLK), BLK)
            high, low = split(block)
            band[0, at_rows, at_lanes] = high
            band[1, at_rows, at_lanes] = low
        return 0

    lax.fori_loop(0, NBLK, fill_band, 0)

    def turn_band(i, _):
        at_lanes = pl.ds(pl.multiple_of(i * 2 * BLK, 2 * BLK), 2 * BLK)
        for part in range(2):
            turned_band[part * LEAF : (part + 1) * LEAF, at_lanes] = mm(
                turned[...], band[part, :, at_lanes]
            ).astype(BF16)
        return 0

    lax.fori_loop(0, 3 * LEAF // (2 * BLK), turn_band, 0)

    loads[6].wait()
    spread = mm(turned[...], wide(u_v[...])).astype(BF16)
    far_w[0:LEAF, :] = spread[:, :R]
    far_w[LEAF : 2 * LEAF, :] = spread[:, R:]

    def one_hot(perm):
        column = jnp.broadcast_to(perm.astype(F32), (R, LEAF)).T
        lane = lax.broadcasted_iota(jnp.int32, (LEAF, R), 1).astype(F32)
        for i in range(LEAF // R):
            straight[:, i * R : (i + 1) * R] = jnp.where(
                column == lane + float(i * R), 1.0, 0.0
            ).astype(BF16)

    def fold(place, perm, factor):
        one_hot(perm)

        def fold_rows(i, _):
            at_rows = pl.ds(pl.multiple_of(i * 2 * BLK, 2 * BLK), 2 * BLK)
            got = mm(turned_band[at_rows, place * LEAF : (place + 1) * LEAF], straight[...])
            near_w[place, at_rows, :] = (got * factor).astype(BF16)
            return 0

        lax.fori_loop(0, 2 * LEAF // (2 * BLK), fold_rows, 0)

    def near_part(place, x):
        r = halves(mm(near_w[place], wide(x)))
        return r[:LEAF] + r[LEAF:]

    def up(m, nodes):
        n = len(nodes) // 2 * nodes[0].shape[0]
        lh, ll = split(rows(nodes[0::2]))
        rh, rl = split(rows(nodes[1::2]))
        to_left = halves(mm(lanes([rh, rl]), coup_w[m, 0]))
        to_right = halves(mm(lanes([lh, ll]), coup_w[m, 1]))
        if m == levels - 1:
            return (to_left, to_right), None
        both = rows([lanes([lh, rh]), lanes([ll, rl])])
        parent = halves(mm(both, up_w[m]))
        parent = parent[:n] + parent[n:]
        return (to_left, to_right), cut(parent, len(nodes) // 2)

    def cut(x, parts):
        each = x.shape[0] // parts
        return [x[i * each : (i + 1) * each] for i in range(parts)]

    def down(m, coup, nodes):
        d = halves(mm(wide(rows(nodes)), down_w[m]))
        lefts = cut(coup[0] + d[:, :R], len(nodes))
        rights = cut(coup[1] + d[:, R:], len(nodes))
        return [node for pair in zip(lefts, rights) for node in pair]

    lz, lx, ly = log2(NZ), log2(nxc), log2(NY)
    coups = [None] * levels
    for k in range(1, NZ):
        z_copy(k).wait_recv()
    nodes = [z_in[k] for k in range(NZ)]
    for m in range(lz):
        coups[m], nodes = up(m, nodes)
    x_out[...] = nodes[0]

    def x_copy(k):
        to = lax.rem(xc + k, nxc)
        return remote(
            x_out.at[pl.ds(to * cx, cx), :], x_in.at[xc], x_send.at[k], x_recv.at[k], x_dev(to)
        )

    for k in range(1, nxc):
        x_copy(k).start()
    x_in[xc] = x_out[pl.ds(xc * cx, cx), :]
    fold(1, perm_row, 1.0)
    for k in range(1, nxc):
        x_copy(k).wait_recv()
    nodes = [x_in[k] for k in range(nxc)]
    for m in range(lz, lz + lx):
        coups[m], nodes = up(m, nodes)
    y_out[...] = nodes[0]

    def y_copy(k):
        to = lax.rem(y + k, NY)
        return remote(y_out, y_in.at[y], y_send.at[k], y_recv.at[k], y_dev(to))

    for k in range(1, NY):
        y_copy(k).start()
    y_in[y] = y_out[...]
    halo_perm(0).wait_recv()
    fold(0, perm_in[0], jnp.where(leaf > 0, 1.0, 0.0).astype(F32))
    for k in range(1, NY):
        y_copy(k).wait_recv()
    nodes = [y_in[k] for k in range(NY)]
    for m in range(lz + lx, levels):
        coups[m], nodes = up(m, nodes)
    nodes = [coups[levels - 1][0], coups[levels - 1][1]]
    for m in range(levels - 2, lz + lx - 1, -1):
        nodes = down(m, coups[m], nodes)
    for k in range(NY):
        top[k] = nodes[k]
    nodes = [top[y]]
    for m in range(lz + lx - 1, lz - 1, -1):
        nodes = down(m, coups[m], nodes)
    for k in range(nxc):
        xr_out[k] = nodes[k]

    def xr_copy(k):
        to = lax.rem(xc + k, nxc)
        return remote(xr_out.at[to], xr_in.at[xc], xr_send.at[k], xr_recv.at[k], x_dev(to))

    for k in range(1, nxc):
        xr_copy(k).start()
    xr_in[xc] = xr_out[xc]
    halo_perm(1).wait_recv()
    fold(2, perm_in[1], jnp.where(leaf < leaves - 1, 1.0, 0.0).astype(F32))
    for k in range(1, nxc):
        xr_copy(k).wait_recv()
    nodes = [rows([xr_in[k] for k in range(nxc)])]
    for m in range(lz - 1, -1, -1):
        nodes = down(m, coups[m], nodes)
    for k in range(NZ):
        zr_out[k] = nodes[k]

    def zr_copy(k):
        to = lax.rem(z + k, NZ)
        return remote(zr_out.at[to], zr_in.at[z], zr_send.at[k], zr_recv.at[k], z_dev(to))

    for k in range(1, NZ):
        zr_copy(k).start()
    zr_in[z] = zr_out[z]

    for c in range(chunks):
        total[c] = near_part(1, x_v[:, c * CW : (c + 1) * CW])
    for c in range(chunks):
        for side in range(2):
            halo(side, c).wait_recv()
            total[c] = total[c] + near_part(2 * side, raw[side, c])

    for k in range(1, NZ):
        zr_copy(k).wait_recv()
    for c in range(chunks):
        each = CW // cz if CW >= cz else 1
        if CW >= cz:
            e = rows([zr_in[c * each + i] for i in range(each)])
        else:
            e = zr_in[c * CW // cz, c * CW % cz : c * CW % cz + CW]
        r = halves(mm(far_w[...], wide(e.T)))
        out_v[c] = total[c] + r[:LEAF] + r[LEAF:]
        pltpu.make_async_copy(
            out_v.at[c], out_hbm.at[:, pl.ds(c * CW, CW)], store_sem.at[c]
        ).start()
    for c in range(chunks):
        pltpu.make_async_copy(
            out_v.at[c], out_hbm.at[:, pl.ds(c * CW, CW)], store_sem.at[c]
        ).wait()

    for k in range(1, NZ):
        z_copy(k).wait_send()
        zr_copy(k).wait_send()
    for k in range(1, nxc):
        x_copy(k).wait_send()
        xr_copy(k).wait_send()
    for k in range(1, NY):
        y_copy(k).wait_send()
    for side in range(2):
        halo_perm(side).wait_send()
        for chunk in range(chunks):
            halo(side, chunk).wait_send()


def per_device(
    columns, col_basis, row_basis, order_perm, near_blocks, band_offsets, transfer, coupling
):
    nxc = NX * NC
    levels = coupling.shape[0]
    chunks = NRHS // CW
    cz = NRHS // NZ
    cx = cz // nxc
    transfer = transfer.reshape(levels - 1, 2 * R, R)
    vmem = pltpu.VMEM
    dma = pltpu.SemaphoreType.DMA
    return pl.pallas_call(
        kernel,
        out_shape=jax.ShapeDtypeStruct((LEAF, NRHS), F32),
        in_specs=[pl.BlockSpec(memory_space=pl.ANY)] * 8,
        out_specs=pl.BlockSpec(memory_space=pl.ANY),
        scratch_shapes=[
            vmem((LEAF, NRHS), F32),
            vmem((LEAF, R), F32),
            vmem((LEAF, R), F32),
            vmem((1, LEAF), jnp.int32),
            vmem((NBLK, NBAND, BLK, BLK), F32),
            pltpu.SMEM((NBLK, NBAND), jnp.int32),
            vmem((levels - 1, 2 * R, R), F32),
            vmem((levels, R, R), F32),
            vmem((levels - 1, 2 * R, 2 * R), BF16),
            vmem((levels - 1, 2 * R, 4 * R), BF16),
            vmem((levels, 2, 2 * R, 2 * R), BF16),
            vmem((2, LEAF, 3 * LEAF), BF16),
            vmem((2 * LEAF, 3 * LEAF), BF16),
            vmem((3, 2 * LEAF, LEAF), BF16),
            vmem((2 * LEAF, R), BF16),
            vmem((LEAF, LEAF), BF16),
            vmem((LEAF, LEAF), BF16),
            vmem((chunks, LEAF, CW), F32),
            vmem((chunks, LEAF, CW), F32),
            vmem((NRHS, R), F32),
            vmem((NZ, cz, R), F32),
            vmem((cz, R), F32),
            vmem((nxc, cx, R), F32),
            vmem((cx, R), F32),
            vmem((NY, cx, R), F32),
            vmem((NY, cx, R), F32),
            vmem((nxc, cx, R), F32),
            vmem((nxc, cx, R), F32),
            vmem((NZ, cz, R), F32),
            vmem((NZ, cz, R), F32),
            vmem((2, chunks, LEAF, CW), F32),
            vmem((2, 1, LEAF), jnp.int32),
            dma((8,)),
            dma((chunks,)),
            dma((NZ,)),
            dma((NZ,)),
            dma((nxc,)),
            dma((nxc,)),
            dma((NY,)),
            dma((NY,)),
            dma((nxc,)),
            dma((nxc,)),
            dma((NZ,)),
            dma((NZ,)),
            dma((2, chunks)),
            dma((2, chunks)),
            dma((2,)),
            dma((2,)),
        ],
        compiler_params=pltpu.CompilerParams(
            collective_id=0, has_side_effects=True, vmem_limit_bytes=58 * 1024 * 1024
        ),
    )(
        columns, col_basis, row_basis, order_perm, near_blocks, band_offsets, transfer, coupling
    )


def solution(mesh):
    placed = (
        P(("gx", "gy"), None),
        P(("gx", "gy"), None),
        P(("gx", "gy"), None),
        P(("gx", "gy"), None),
        P(("gx", "gy"), None, None, None),
        P(("gx", "gy"), None),
        P(),
        P(),
    )
    return jax.shard_map(
        per_device, mesh=mesh, in_specs=placed, out_specs=P(("gx", "gy"), None), check_vma=False
    )
```

time: 185 us -> 68.2 us (0.37)
  the two profiles are of different devices: /device:TPU:57 before, /device:TPU:1 now
where the time goes in v1:
time: 68.2 us; the launch traced here: 68.1 us
  Pallas kernels  65.8 us (96%)
  local copies, waits for them, and re-layouts  2.26 us (3%)
    pallas_call x1, Pallas kernels, per_device(): pl.pallas_call(kernel, out_shape=jax.ShapeDtypeStruct((LEAF, NRHS), F32),...  65.8 us
    unnamed x1, local copies, waits for them, and re-layouts  2.26 us

profile of v1, /device:TPU:1, one launch (start us, length us, event | category | flops | bytes accessed | tf_op | source)
XLA Modules:
  0.0 68.1 jit_solution(14457026476505408191)
XLA Ops:
  0.0 65.8 %shard_map.82 = f32[512,512]{1,0:T(8,128)} custom-call(f32[512,512]{1,0:T(8,128)} %x_hbm.1, f32[512,128]{1,0:T(8,128)} %v_hbm.1, f32[512,128]{1,0:T(8,128)} %u_hbm.1, s32[1,512]{1,0:T(1,128)} %perm_hbm.1, f32[4,5,128,128]{3,2,1,0:T(8,128)} %near_hbm.1, s32[4,5]{1,0:T(4,128)} %off_hbm.1, f32[8,256,128]{2,1,0:T(8,128)} %bitcast.1, f32[9,128,128]{2,1,0:T(8,128)} %coupling_hbm.1), custom_call_target="tpu_custom_call" | custom-call | tf_op jit(solution)/shard_map/pallas_call | solution.py:405
  65.8 2.3 %copy.10 = f32[512,512]{1,0:T(8,128)} copy(f32[512,512]{1,0:T(8,128)} %shard_map.82) | data formatting | bytes 2097152

commit v2 on v1

--- a/solution.py
+++ b/solution.py
@@ -56,34 +56,29 @@
 
 
 def kernel(
-    x_hbm, v_hbm, u_hbm, perm_hbm, near_hbm, off_hbm, transfer_hbm, coupling_hbm, out_hbm,
+    x_hbm, v_hbm, u_hbm, perm_hbm, near_hbm, off_hbm, transfer_hbm, coupling_hbm, product,
     x_v, v_v, u_v, perm_v, near_v, off_s, transfer_v, coupling_v,
-    up_w, down_w, coup_w, band, turned_band, near_w, far_w, turned, straight, total, out_v,
-    skel, z_in, x_out, x_in, y_out, y_in, top, xr_out, xr_in, zr_out, zr_in,
+    up_w, down_w, coup_w, band, turned_band, near_w, far_w, turned, straight, total,
+    skel, up_in, y_out, y_in, top, down_out, down_in,
     raw, perm_in,
-    load_sem, store_sem,
-    z_send, z_recv, x_send, x_recv, y_send, y_recv, xr_send, xr_recv, zr_send, zr_recv,
+    load_sem,
+    up_send, up_recv, y_send, y_recv, down_send, down_recv,
     halo_send, halo_recv, perm_send, perm_recv,
 ):
-    nxc = NX * NC
     gx = lax.axis_index("gx")
     gy = lax.axis_index("gy")
     y, core = lax.div(gx, NC), lax.rem(gx, NC)
-    xx, z = lax.div(gy, NZ), lax.rem(gy, NZ)
     along = NX * NZ
-    leaves = along * NC * NY
+    team = along * NC
+    leaves = team * NY
     leaf = gx * along + gy
-    xc = core * NX + xx
+    place = core * along + gy
     levels = coupling_hbm.shape[0]
     chunks = NRHS // CW
-    cz = NRHS // NZ
-    cx = cz // nxc
-
-    def z_dev(k):
-        return (gx, xx * NZ + k)
-
-    def x_dev(k):
-        return (y * NC + lax.div(k, NX), lax.rem(k, NX) * NZ + z)
+    share = NRHS // team
+
+    def team_dev(k):
+        return (y * NC + lax.div(k, along), lax.rem(k, along))
 
     def y_dev(k):
         return (k * NC + core, gy)
@@ -119,14 +114,19 @@
 
     barrier = pltpu.get_barrier_semaphore()
     greeted = (
-        [z_dev(lax.rem(z + k, NZ)) for k in range(1, NZ)]
-        + [x_dev(lax.rem(xc + k, nxc)) for k in range(1, nxc)]
-        + [y_dev(lax.rem(y + k, NY)) for k in range(1, NY)]
+        [y_dev(lax.rem(y + k, NY)) for k in range(1, NY)]
         + [left, right]
     )
     for dev in greeted:
         pl.semaphore_signal(barrier, inc=1, device_id=dev, device_id_type=MESH)
-    pl.semaphore_wait(barrier, len(greeted))
+
+    def greet(k, _):
+        dev = team_dev(lax.rem(place + k, team))
+        pl.semaphore_signal(barrier, inc=1, device_id=dev, device_id_type=MESH)
+        return 0
+
+    lax.fori_loop(1, team, greet, 0)
+    pl.semaphore_wait(barrier, len(greeted) + team - 1)
 
     def halo(side, chunk):
         return remote(
@@ -142,9 +142,14 @@
             perm_hbm, perm_in.at[side], perm_send.at[side], perm_recv.at[side], (right, left)[side]
         )
 
+    def send_halo(*which):
+        for chunk in which:
+            for side in range(2):
+                halo(side, chunk).start()
+
     for side in range(2):
         halo_perm(side).start()
-        halo(side, 0).start()
+    send_halo(0)
 
     loads[0].wait()
     perm_row = perm_v[...]
@@ -161,18 +166,20 @@
         s = s[:R] + s[R:]
         skel[c * CW : (c + 1) * CW, :] = s.T
 
-    def z_copy(k):
-        to = lax.rem(z + k, NZ)
-        return remote(
-            skel.at[pl.ds(to * cz, cz), :], z_in.at[z], z_send.at[k], z_recv.at[k], z_dev(to)
-        )
-
-    for k in range(1, NZ):
-        z_copy(k).start()
-    z_in[z] = skel[pl.ds(z * cz, cz), :]
-    for chunk in range(1, chunks):
-        for side in range(2):
-            halo(side, chunk).start()
+    def up_start(k, _):
+        to = lax.rem(place + k, team)
+        remote(
+            skel.at[pl.ds(pl.multiple_of(to * share, share), share), :],
+            up_in.at[place], up_send, up_recv, team_dev(to),
+        ).start()
+        return 0
+
+    def all_but_one(buf, sem, n):
+        return pltpu.make_async_copy(buf.at[pl.ds(0, n - 1)], buf.at[pl.ds(0, n - 1)], sem)
+
+    lax.fori_loop(1, team, up_start, 0)
+    send_halo(1)
+    up_in[place] = skel[pl.ds(pl.multiple_of(place * share, share), share), :]
 
     loads[3].wait()
     loads[4].wait()
@@ -238,19 +245,19 @@
                 column == lane + float(i * R), 1.0, 0.0
             ).astype(BF16)
 
-    def fold(place, perm, factor):
+    def fold(which, perm, factor):
         one_hot(perm)
 
         def fold_rows(i, _):
             at_rows = pl.ds(pl.multiple_of(i * 2 * BLK, 2 * BLK), 2 * BLK)
-            got = mm(turned_band[at_rows, place * LEAF : (place + 1) * LEAF], straight[...])
-            near_w[place, at_rows, :] = (got * factor).astype(BF16)
+            got = mm(turned_band[at_rows, which * LEAF : (which + 1) * LEAF], straight[...])
+            near_w[which, at_rows, :] = (got * factor).astype(BF16)
             return 0
 
         lax.fori_loop(0, 2 * LEAF // (2 * BLK), fold_rows, 0)
 
-    def near_part(place, x):
-        r = halves(mm(near_w[place], wide(x)))
+    def near_part(which, x):
+        r = halves(mm(near_w[which], wide(x)))
         return r[:LEAF] + r[LEAF:]
 
     def up(m, nodes):
@@ -276,82 +283,46 @@
         rights = cut(coup[1] + d[:, R:], len(nodes))
         return [node for pair in zip(lefts, rights) for node in pair]
 
-    lz, lx, ly = log2(NZ), log2(nxc), log2(NY)
+    within = log2(team)
     coups = [None] * levels
-    for k in range(1, NZ):
-        z_copy(k).wait_recv()
-    nodes = [z_in[k] for k in range(NZ)]
-    for m in range(lz):
-        coups[m], nodes = up(m, nodes)
-    x_out[...] = nodes[0]
-
-    def x_copy(k):
-        to = lax.rem(xc + k, nxc)
-        return remote(
-            x_out.at[pl.ds(to * cx, cx), :], x_in.at[xc], x_send.at[k], x_recv.at[k], x_dev(to)
-        )
-
-    for k in range(1, nxc):
-        x_copy(k).start()
-    x_in[xc] = x_out[pl.ds(xc * cx, cx), :]
-    fold(1, perm_row, 1.0)
-    for k in range(1, nxc):
-        x_copy(k).wait_recv()
-    nodes = [x_in[k] for k in range(nxc)]
-    for m in range(lz, lz + lx):
+    all_but_one(up_in, up_recv, team).wait()
+    send_halo(2, 3)
+    nodes = [up_in[k] for k in range(team)]
+    for m in range(within):
         coups[m], nodes = up(m, nodes)
     y_out[...] = nodes[0]
-
-    def y_copy(k):
+    for k in range(1, NY):
         to = lax.rem(y + k, NY)
-        return remote(y_out, y_in.at[y], y_send.at[k], y_recv.at[k], y_dev(to))
-
-    for k in range(1, NY):
-        y_copy(k).start()
+        remote(y_out, y_in.at[y], y_send, y_recv, y_dev(to)).start()
     y_in[y] = y_out[...]
-    halo_perm(0).wait_recv()
-    fold(0, perm_in[0], jnp.where(leaf > 0, 1.0, 0.0).astype(F32))
-    for k in range(1, NY):
-        y_copy(k).wait_recv()
+    fold(1, perm_row, 1.0)
+    all_but_one(y_in, y_recv, NY).wait()
     nodes = [y_in[k] for k in range(NY)]
-    for m in range(lz + lx, levels):
+    for m in range(within, levels):
         coups[m], nodes = up(m, nodes)
     nodes = [coups[levels - 1][0], coups[levels - 1][1]]
-    for m in range(levels - 2, lz + lx - 1, -1):
+    for m in range(levels - 2, within - 1, -1):
         nodes = down(m, coups[m], nodes)
     for k in range(NY):
         top[k] = nodes[k]
     nodes = [top[y]]
-    for m in range(lz + lx - 1, lz - 1, -1):
+    for m in range(within - 1, -1, -1):
         nodes = down(m, coups[m], nodes)
-    for k in range(nxc):
-        xr_out[k] = nodes[k]
-
-    def xr_copy(k):
-        to = lax.rem(xc + k, nxc)
-        return remote(xr_out.at[to], xr_in.at[xc], xr_send.at[k], xr_recv.at[k], x_dev(to))
-
-    for k in range(1, nxc):
-        xr_copy(k).start()
-    xr_in[xc] = xr_out[xc]
-    halo_perm(1).wait_recv()
+    for k in range(team):
+        down_out[k] = nodes[k]
+
+    def down_start(k, _):
+        to = lax.rem(place + k, team)
+        remote(down_out.at[to], down_in.at[place], down_send, down_recv, team_dev(to)).start()
+        return 0
+
+    lax.fori_loop(1, team, down_start, 0)
+    down_in[place] = down_out[place]
+
+    for side in range(2):
+        halo_perm(side).wait_recv()
+    fold(0, perm_in[0], jnp.where(leaf > 0, 1.0, 0.0).astype(F32))
     fold(2, perm_in[1], jnp.where(leaf < leaves - 1, 1.0, 0.0).astype(F32))
-    for k in range(1, nxc):
-        xr_copy(k).wait_recv()
-    nodes = [rows([xr_in[k] for k in range(nxc)])]
-    for m in range(lz - 1, -1, -1):
-        nodes = down(m, coups[m], nodes)
-    for k in range(NZ):
-        zr_out[k] = nodes[k]
-
-    def zr_copy(k):
-        to = lax.rem(z + k, NZ)
-        return remote(zr_out.at[to], zr_in.at[z], zr_send.at[k], zr_recv.at[k], z_dev(to))
-
-    for k in range(1, NZ):
-        zr_copy(k).start()
-    zr_in[z] = zr_out[z]
-
     for c in range(chunks):
         total[c] = near_part(1, x_v[:, c * CW : (c + 1) * CW])
     for c in range(chunks):
@@ -359,32 +330,14 @@
             halo(side, c).wait_recv()
             total[c] = total[c] + near_part(2 * side, raw[side, c])
 
-    for k in range(1, NZ):
-        zr_copy(k).wait_recv()
+    all_but_one(down_in, down_recv, team).wait()
+    expanded = down_in[...].reshape(NRHS, R)
     for c in range(chunks):
-        each = CW // cz if CW >= cz else 1
-        if CW >= cz:
-            e = rows([zr_in[c * each + i] for i in range(each)])
-        else:
-            e = zr_in[c * CW // cz, c * CW % cz : c * CW % cz + CW]
-        r = halves(mm(far_w[...], wide(e.T)))
-        out_v[c] = total[c] + r[:LEAF] + r[LEAF:]
-        pltpu.make_async_copy(
-            out_v.at[c], out_hbm.at[:, pl.ds(c * CW, CW)], store_sem.at[c]
-        ).start()
-    for c in range(chunks):
-        pltpu.make_async_copy(
-            out_v.at[c], out_hbm.at[:, pl.ds(c * CW, CW)], store_sem.at[c]
-        ).wait()
-
-    for k in range(1, NZ):
-        z_copy(k).wait_send()
-        zr_copy(k).wait_send()
-    for k in range(1, nxc):
-        x_copy(k).wait_send()
-        xr_copy(k).wait_send()
-    for k in range(1, NY):
-        y_copy(k).wait_send()
+        r = halves(mm(far_w[...], wide(expanded[c * CW : (c + 1) * CW].T)))
+        product[:, c * CW : (c + 1) * CW] = total[c] + r[:LEAF] + r[LEAF:]
+    all_but_one(up_in, up_send, team).wait()
+    all_but_one(down_in, down_send, team).wait()
+    all_but_one(y_in, y_send, NY).wait()
     for side in range(2):
         halo_perm(side).wait_send()
         for chunk in range(chunks):
@@ -394,19 +347,18 @@
 def per_device(
     columns, col_basis, row_basis, order_perm, near_blocks, band_offsets, transfer, coupling
 ):
-    nxc = NX * NC
     levels = coupling.shape[0]
     chunks = NRHS // CW
-    cz = NRHS // NZ
-    cx = cz // nxc
+    team = NX * NC * NZ
+    share = NRHS // team
     transfer = transfer.reshape(levels - 1, 2 * R, R)
     vmem = pltpu.VMEM
     dma = pltpu.SemaphoreType.DMA
     return pl.pallas_call(
         kernel,
-        out_shape=jax.ShapeDtypeStruct((LEAF, NRHS), F32),
+        out_shape=vmem((LEAF, NRHS), F32),
         in_specs=[pl.BlockSpec(memory_space=pl.ANY)] * 8,
-        out_specs=pl.BlockSpec(memory_space=pl.ANY),
+        out_specs=pl.BlockSpec(memory_space=pltpu.VMEM),
         scratch_shapes=[
             vmem((LEAF, NRHS), F32),
             vmem((LEAF, R), F32),
@@ -426,32 +378,22 @@
             vmem((LEAF, LEAF), BF16),
             vmem((LEAF, LEAF), BF16),
             vmem((chunks, LEAF, CW), F32),
-            vmem((chunks, LEAF, CW), F32),
             vmem((NRHS, R), F32),
-            vmem((NZ, cz, R), F32),
-            vmem((cz, R), F32),
-            vmem((nxc, cx, R), F32),
-            vmem((cx, R), F32),
-            vmem((NY, cx, R), F32),
-            vmem((NY, cx, R), F32),
-            vmem((nxc, cx, R), F32),
-            vmem((nxc, cx, R), F32),
-            vmem((NZ, cz, R), F32),
-            vmem((NZ, cz, R), F32),
+            vmem((team, share, R), F32),
+            vmem((share, R), F32),
+            vmem((NY, share, R), F32),
+            vmem((NY, share, R), F32),
+            vmem((team, share, R), F32),
+            vmem((team, share, R), F32),
             vmem((2, chunks, LEAF, CW), F32),
             vmem((2, 1, LEAF), jnp.int32),
             dma((8,)),
-            dma((chunks,)),
-            dma((NZ,)),
-            dma((NZ,)),
-            dma((nxc,)),
-            dma((nxc,)),
-            dma((NY,)),
-            dma((NY,)),
-            dma((nxc,)),
-            dma((nxc,)),
-            dma((NZ,)),
-            dma((NZ,)),
+            dma,
+            dma,
+            dma,
+            dma,
+            dma,
+            dma,
             dma((2, chunks)),
             dma((2, chunks)),
             dma((2,)),

time: 68.2 us -> 56.5 us (0.83)
  the two profiles are of different devices: /device:TPU:1 before, /device:TPU:8 now
where the time goes in v2:
time: 56.5 us; the launch traced here: 56.4 us
  Pallas kernels  55.4 us (98%)
  local copies, waits for them, and re-layouts  0.97 us (2%)
    pallas_call x1, Pallas kernels, per_device(): pl.pallas_call(kernel, out_shape=vmem((LEAF, NRHS), F32), in_specs=[pl.Bl...  55.4 us

profile of v2, /device:TPU:8, one launch (start us, length us, event | category | flops | bytes accessed | tf_op | source)
XLA Modules:
  0.0 56.4 jit_solution(13850253502276147888)
XLA Ops:
  0.0 55.4 %shard_map.82 = f32[512,512]{1,0:T(8,128)S(1)} custom-call(f32[512,512]{1,0:T(8,128)} %x_hbm.1, f32[512,128]{1,0:T(8,128)} %v_hbm.1, f32[512,128]{1,0:T(8,128)} %u_hbm.1, s32[1,512]{1,0:T(1,128)} %perm_hbm.1, f32[4,5,128,128]{3,2,1,0:T(8,128)} %near_hbm.1, s32[4,5]{1,0:T(4,128)} %off_hbm.1, f32[8,256,128]{2,1,0:T(8,128)} %bitcast.1, f32[9,128,128]{2,1,0:T(8,128)} %coupling_hbm.1), custom_call_target="tpu_custom_call" | custom-call | tf_op jit(solution)/shard_map/pallas_call | solution.py:357
  55.4 1.0 %copy.10 = f32[512,512]{1,0:T(8,128)} copy(f32[512,512]{1,0:T(8,128)S(1)} %shard_map.82) | data formatting | bytes 2097152

commit v3 on v2

--- a/solution.py
+++ b/solution.py
@@ -178,7 +178,7 @@
         return pltpu.make_async_copy(buf.at[pl.ds(0, n - 1)], buf.at[pl.ds(0, n - 1)], sem)
 
     lax.fori_loop(1, team, up_start, 0)
-    send_halo(1)
+    send_halo(1, 2)
     up_in[place] = skel[pl.ds(pl.multiple_of(place * share, share), share), :]
 
     loads[3].wait()
@@ -233,9 +233,7 @@
     lax.fori_loop(0, 3 * LEAF // (2 * BLK), turn_band, 0)
 
     loads[6].wait()
-    spread = mm(turned[...], wide(u_v[...])).astype(BF16)
-    far_w[0:LEAF, :] = spread[:, :R]
-    far_w[LEAF : 2 * LEAF, :] = spread[:, R:]
+    far_w[...] = mm(turned[...], wide(u_v[...])).astype(BF16)
 
     def one_hot(perm):
         column = jnp.broadcast_to(perm.astype(F32), (R, LEAF)).T
@@ -260,18 +258,20 @@
         r = halves(mm(near_w[which], wide(x)))
         return r[:LEAF] + r[LEAF:]
 
-    def up(m, nodes):
-        n = len(nodes) // 2 * nodes[0].shape[0]
-        lh, ll = split(rows(nodes[0::2]))
-        rh, rl = split(rows(nodes[1::2]))
+    def pairs(nodes):
+        return split(rows(nodes[0::2])) + split(rows(nodes[1::2]))
+
+    def couple(m, pair):
+        lh, ll, rh, rl = pair
         to_left = halves(mm(lanes([rh, rl]), coup_w[m, 0]))
         to_right = halves(mm(lanes([lh, ll]), coup_w[m, 1]))
-        if m == levels - 1:
-            return (to_left, to_right), None
-        both = rows([lanes([lh, rh]), lanes([ll, rl])])
-        parent = halves(mm(both, up_w[m]))
-        parent = parent[:n] + parent[n:]
-        return (to_left, to_right), cut(parent, len(nodes) // 2)
+        return to_left, to_right
+
+    def up(m, pair):
+        lh, ll, rh, rl = pair
+        n = lh.shape[0]
+        parent = halves(mm(rows([lanes([lh, rh]), lanes([ll, rl])]), up_w[m]))
+        return cut(parent[:n] + parent[n:], n // share)
 
     def cut(x, parts):
         each = x.shape[0] // parts
@@ -286,20 +286,27 @@
     within = log2(team)
     coups = [None] * levels
     all_but_one(up_in, up_recv, team).wait()
-    send_halo(2, 3)
+    send_halo(3)
     nodes = [up_in[k] for k in range(team)]
+    below = []
     for m in range(within):
-        coups[m], nodes = up(m, nodes)
+        below.append(pairs(nodes))
+        nodes = up(m, below[m])
     y_out[...] = nodes[0]
     for k in range(1, NY):
         to = lax.rem(y + k, NY)
         remote(y_out, y_in.at[y], y_send, y_recv, y_dev(to)).start()
     y_in[y] = y_out[...]
+    for m in range(within - 1, -1, -1):
+        coups[m] = couple(m, below[m])
     fold(1, perm_row, 1.0)
     all_but_one(y_in, y_recv, NY).wait()
     nodes = [y_in[k] for k in range(NY)]
     for m in range(within, levels):
-        coups[m], nodes = up(m, nodes)
+        pair = pairs(nodes)
+        if m < levels - 1:
+            nodes = up(m, pair)
+        coups[m] = couple(m, pair)
     nodes = [coups[levels - 1][0], coups[levels - 1][1]]
     for m in range(levels - 2, within - 1, -1):
         nodes = down(m, coups[m], nodes)
@@ -333,8 +340,8 @@
     all_but_one(down_in, down_recv, team).wait()
     expanded = down_in[...].reshape(NRHS, R)
     for c in range(chunks):
-        r = halves(mm(far_w[...], wide(expanded[c * CW : (c + 1) * CW].T)))
-        product[:, c * CW : (c + 1) * CW] = total[c] + r[:LEAF] + r[LEAF:]
+        e = wide(expanded[c * CW : (c + 1) * CW].T)
+        product[:, c * CW : (c + 1) * CW] = total[c] + halves(mm(far_w[...], rows([e, e])))
     all_but_one(up_in, up_send, team).wait()
     all_but_one(down_in, down_send, team).wait()
     all_but_one(y_in, y_send, NY).wait()
@@ -374,7 +381,7 @@
             vmem((2, LEAF, 3 * LEAF), BF16),
             vmem((2 * LEAF, 3 * LEAF), BF16),
             vmem((3, 2 * LEAF, LEAF), BF16),
-            vmem((2 * LEAF, R), BF16),
+            vmem((LEAF, 2 * R), BF16),
             vmem((LEAF, LEAF), BF16),
             vmem((LEAF, LEAF), BF16),
             vmem((chunks, LEAF, CW), F32),

time: 56.5 us -> 56 us (level)
  no operation moved by 1% of the time
where the time goes in v3:
time: 56 us; the launch traced here: 55.9 us
  Pallas kernels  54.9 us (98%)
  local copies, waits for them, and re-layouts  0.97 us (2%)
    pallas_call x1, Pallas kernels, per_device(): pl.pallas_call(kernel, out_shape=vmem((LEAF, NRHS), F32), in_specs=[pl.Bl...  54.9 us

profile of v3, /device:TPU:8, one launch (start us, length us, event | category | flops | bytes accessed | tf_op | source)
XLA Modules:
  0.0 55.9 jit_solution(532593834885479258)
XLA Ops:
  0.0 54.9 %shard_map.82 = f32[512,512]{1,0:T(8,128)S(1)} custom-call(f32[512,512]{1,0:T(8,128)} %x_hbm.1, f32[512,128]{1,0:T(8,128)} %v_hbm.1, f32[512,128]{1,0:T(8,128)} %u_hbm.1, s32[1,512]{1,0:T(1,128)} %perm_hbm.1, f32[4,5,128,128]{3,2,1,0:T(8,128)} %near_hbm.1, s32[4,5]{1,0:T(4,128)} %off_hbm.1, f32[8,256,128]{2,1,0:T(8,128)} %bitcast.1, f32[9,128,128]{2,1,0:T(8,128)} %coupling_hbm.1), custom_call_target="tpu_custom_call" | custom-call | tf_op jit(solution)/shard_map/pallas_call | solution.py:364
  54.9 1.0 %copy.10 = f32[512,512]{1,0:T(8,128)} copy(f32[512,512]{1,0:T(8,128)S(1)} %shard_map.82) | data formatting | bytes 2097152
